TPU v7x, 256 devices: a whole 4x4x8 slice. The times are simulated.
256 devices in a mesh: curve: 64 (over y, z, core), band: 4 (over x).
Axes of the slice: x: 4, y: 4, z: 8, core: 2. Of those that a mesh axis runs over, the one named last changes fastest.
Arguments:
- state: float32 [16, 16384, 128], P('band', 'curve'), may hold values from -3 to 3
- blocks: bfloat16 [16384, 4, 128, 128], P('curve', 'band'), may hold values from -0.25 to 0.25
- diag_blocks: bfloat16 [16384, 128, 128], P(('curve', 'band')), may hold values from -1 to 1, as said below
- block_cols: int32 [16384, 4], P('curve', 'band'), may hold values from 0 to 16383, as said below
Outputs:
- updated: float32 [16, 16384, 128], P('band', 'curve')
Inputs may be any that keep to these rules, and one draw needn't show every extreme that they name: `diag_blocks`: every diagonal block is symmetric. `block_cols`: A column is never the row's own patch, and no pair of patches is stored twice, in either order. The owner of patch p is index p // 256 of curve. Of the 256 rows of one index of curve, in each slot exactly 64 have their column on another index: 2 on each of 32 other indices; the columns of the others lie on the own index.
All inputs are finite; a program needn't handle non-finite values.
Results may differ from a plain program's by a relative error of at most 0.0003.
The roundings to bfloat16 on the way count: a program that leaves them out, or rounds other values in their place, can miss the bound.
Values may be sent and summed in bfloat16 or wider, within the bound.
A program may use at most 64 MiB of HBM per device.

v0:
```python
import jax
import jax.numpy as jnp
from jax import lax
from jax.sharding import PartitionSpec as P

CAP = 2
TAYLOR = 16


epsilon = 1e-06
time_step = 0.5
quadratic = 1.0


def nonlinear(field):
    return quadratic * field * field - field * field * field


def phi_weights(alpha_first, beta_first, alpha_second):

    def advance(turn, carry):
        term_one, term_two, total_one, total_two = carry
        factor = time_step / (turn + 1.0)
        next_one = factor * (alpha_first * term_one + beta_first * term_two)
        next_two = factor * (beta_first * term_one + alpha_second * term_two)
        return (next_one, next_two, total_one + next_one, total_two + next_two)

    ones = jnp.ones_like(alpha_first)
    zeros = jnp.zeros_like(alpha_first)
    result = lax.fori_loop(1, TAYLOR, advance, (ones, zeros, ones, zeros))
    return (result[2], result[3])


def routing(block_cols):
    groups = lax.axis_size("curve")
    here = lax.axis_index("curve")
    patch_rows = block_cols.shape[0]
    columns = block_cols[:, 0]
    owner = columns // patch_rows
    target = columns % patch_rows
    remote = owner != here
    peers = jnp.arange(groups, dtype=jnp.int32)
    member = ((owner[:, None] == peers[None, :]) & remote[:, None]).astype(jnp.int32)
    rank = jnp.sum(jnp.cumsum(member, axis=0) * member, axis=1) - 1
    bucket = jnp.where(remote, owner * CAP + rank, groups * CAP)
    pick = jnp.where(remote, patch_rows + owner * CAP + rank, target)
    wanted = jnp.full((groups * CAP + 1,), -1, jnp.int32).at[bucket].set(target)
    asked = lax.all_to_all(
        wanted[:-1].reshape(groups, CAP), "curve", split_axis=0, concat_axis=0, tiled=True
    )
    asked_flat = asked.reshape(-1)
    return (remote, target, bucket, pick, jnp.maximum(asked_flat, 0), asked_flat >= 0)


def local_product(whole, blocks, diag_blocks, plan):
    remote, target, bucket, pick, asked_index, asked_valid = plan
    groups = lax.axis_size("curve")
    vectors, patch_rows, node_count = whole.shape
    reply = whole[:, asked_index, :].reshape(vectors, groups, CAP, node_count)
    arrived = lax.all_to_all(reply, "curve", split_axis=1, concat_axis=1, tiled=True)
    pool = jnp.concatenate([whole, arrived.reshape(vectors, groups * CAP, node_count)], axis=1)
    gathered = pool[:, pick, :]
    stored = blocks[:, 0]
    result = jnp.einsum("rac,vrc->vra", stored, gathered, preferred_element_type=jnp.float32)
    mirrored = jnp.einsum("rac,vra->vrc", stored, whole, preferred_element_type=jnp.float32)
    kept = jnp.where(remote[None, :, None], 0.0, mirrored)
    result = result.at[:, target, :].add(kept)
    outgoing = (
        jnp.zeros((vectors, groups * CAP + 1, node_count), jnp.float32)
        .at[:, bucket, :]
        .add(mirrored)
    )
    outgoing = outgoing[:, :-1, :].reshape(vectors, groups, CAP, node_count)
    returned = lax.all_to_all(outgoing, "curve", split_axis=1, concat_axis=1, tiled=True)
    returned = jnp.where(
        asked_valid[None, :, None], returned.reshape(vectors, groups * CAP, node_count), 0.0
    )
    result = result.at[:, asked_index, :].add(returned)
    quarter = diag_blocks.shape[0]
    start = lax.axis_index("band") * quarter
    own_rows = lax.dynamic_slice_in_dim(whole, start, quarter, 1)
    diagonal = jnp.einsum("rac,vrc->vra", diag_blocks, own_rows, preferred_element_type=jnp.float32)
    current = lax.dynamic_slice_in_dim(result, start, quarter, 1)
    return lax.dynamic_update_slice_in_dim(result, current + diagonal, start, 1)


def operate(vector, blocks, diag_blocks, plan):
    whole = lax.all_gather(vector, "band", axis=0, tiled=True)
    product = lax.psum_scatter(
        local_product(whole, blocks, diag_blocks, plan), "band", scatter_dimension=0, tiled=True
    )
    return product


def body(state, blocks, diag_blocks, block_cols):
    plan = routing(block_cols)
    drive = operate(state.astype(jnp.bfloat16), blocks, diag_blocks, plan) + nonlinear(state)
    drive_norm = lax.psum(jnp.sum(drive * drive, axis=(1, 2)), "curve")
    beta_zero = jnp.sqrt(drive_norm + epsilon)
    first = drive / beta_zero[:, None, None]
    image = operate(first.astype(jnp.bfloat16), blocks, diag_blocks, plan)
    alpha_first = lax.psum(jnp.sum(first * image, axis=(1, 2)), "curve")
    rest = image - alpha_first[:, None, None] * first
    rest_norm = lax.psum(jnp.sum(rest * rest, axis=(1, 2)), "curve")
    beta_first = jnp.sqrt(rest_norm + epsilon)
    second = rest / beta_first[:, None, None]
    image_second = operate(second.astype(jnp.bfloat16), blocks, diag_blocks, plan)
    image_second = image_second - beta_first[:, None, None] * first
    alpha_second = lax.psum(jnp.sum(second * image_second, axis=(1, 2)), "curve")
    weight_one, weight_two = phi_weights(alpha_first, beta_first, alpha_second)
    combined = weight_one[:, None, None] * first + weight_two[:, None, None] * second
    updated = state + time_step * beta_zero[:, None, None] * combined
    return updated


def solution(mesh):
    return jax.shard_map(
        body,
        mesh=mesh,
        in_specs=(
            P("band", "curve", None),
            P("curve", "band", None, None),
            P(("curve", "band"), None, None),
            P("curve", "band"),
        ),
        out_specs=P("band", "curve", None),
        check_vma=False,
    )
```

profile of v0, /device:TPU:1, one launch (start us, length us, event | category | flops | bytes accessed | tf_op | source)
XLA Modules:
  0.0 1115.6 jit_solution(49151905416298263)
XLA Ops:
  6.5 1.9 convert_element_type.21
  11.6 1.4 scatter_custom_fusion
  13.1 22.2 %all_to_all.39 = s32[64,1,2]{2,1,0:T(1,128)S(1)} all-to-all(s32[64,1,2]{2,1,0:T(1,128)S(1)} %bitcast.118), channel_id=1, replica_groups=mesh['curve'=64,'band'=4] {'curve'}, dimensions={0} | all-to-all | bytes 1024 | tf_op jit(solution)/shard_map/all_to_all | solution.py:48
  35.6 3.0 all-gather.4.cloned.1.call-done
  38.6 1.9 copy.35
  40.5 1.5 gather_fusion
  42.0 11.8 %all-to-all-start.1 = ((bf16[16,64,2,128]{3,0,2,1:T(8,128)(2,1)}), bf16[16,64,2,128]{3,0,2,1:T(8,128)(2,1)}, u32[]{:S(2)}, u32[]{:S(2)}) async-start(bf16[16,64,2,128]{3,0,2,1:T(8,128)(2,1)} %bitcast.116), calls=%async_computation.1 | async-start | bytes 1048576 | tf_op jit(solution)/shard_map/all_to_all | solution.py:60
  53.8 8.0 broadcast_select_fusion.6
  61.8 20.7 %scatter_fusion.1 = f32[16,129,128]{2,0,1:T(8,128)S(1)} fusion(f32[16,129,128]{2,0,1:T(8,128)S(1)} %broadcast.188.clone, s32[256]{0:T(256)S(1)} %bitcast.127, f32[256,16,128]{2,1,0:T(8,128)} %get-tuple-element.207), kind=kCustom, calls=%fused_computation.8 | custom fusion | flops 524288 | bytes 6292480 | tf_op jit(solution)/shard_map/scatter-add | solution.py:71
  83.7 10.7 all-to-all-start.2
  94.9 2.4 pad_maximum_fusion
  97.2 3.2 gather_fusion.1
  100.4 9.5 fusion.14
  110.0 31.4 %scatter_fusion = f32[16,256,128]{2,0,1:T(8,128)} fusion(f32[16,256,128]{2,0,1:T(8,128)} %fusion.14, s32[256]{0:T(256)S(1)} %bitcast.123, f32[256,16,128]{2,1,0:T(8,128)} %get-tuple-element.206), kind=kCustom, calls=%fused_computation.7 | custom fusion | flops 524288 | bytes 6292480 | tf_op jit(solution)/shard_map/scatter-add | solution.py:67
  141.4 2.4 bitcast_select_fusion.2
  143.8 16.3 %scatter_fusion.2 = f32[16,256,128]{2,0,1:T(8,128)} fusion(f32[16,256,128]{2,0,1:T(8,128)} %scatter_fusion, s32[128]{0:T(128)S(1)} %reshape.144, f32[128,16,128]{2,1,0:T(8,128)} %bitcast.110), kind=kCustom, calls=%fused_computation.9 | custom fusion | flops 262144 | bytes 3146240 | tf_op jit(solution)/shard_map/scatter-add | solution.py:78
  160.1 3.0 fusion.24
  163.2 3.6 copy.38
  166.8 32.5 %reduce-scatter.4.cloned.1.call-done = f32[4,256,128]{2,1,0:T(8,128)} async-done(((f32[16,256,128]{2,1,0:T(8,128)}), f32[4,256,128]{2,1,0:T(8,128)}) %reduce-scatter.4.cloned.1.call-update) | async-done | bytes 524304 | tf_op jit(solution)/shard_map/reduce_scatter | solution.py:89
  199.3 1.2 multiply_reduce_fusion.3
  200.5 124.5 %psum.28 = f32[4]{0:T(128)S(1)} all-reduce(f32[4]{0:T(128)S(1)} %multiply_reduce_fusion.3), channel_id=1, replica_groups=mesh['curve'=64,'band'=4] {'curve'}, use_global_device_ids=true, to_apply=%region_9.10 | all-reduce | flops 4 | bytes 32 | tf_op jit(solution)/shard_map/psum | solution.py:98
  325.1 1.9 fusion.52
  327.0 22.3 %all-gather.6.cloned.1.call-done = bf16[16,256,128]{2,1,0:T(8,128)(2,1)} async-done(((bf16[4,256,128]{2,1,0:T(8,128)(2,1)}), bf16[16,256,128]{2,1,0:T(8,128)(2,1)}) %all-gather.6.cloned.1.call-update) | async-done | bytes 1048592 | tf_op jit(solution)/shard_map/all_gather | solution.py:88
  349.3 2.9 copy.40
  352.2 2.7 gather_fusion.2
  354.9 11.6 %all-to-all-start.3 = ((bf16[16,64,2,128]{3,0,2,1:T(8,128)(2,1)}), bf16[16,64,2,128]{3,0,2,1:T(8,128)(2,1)S(1)}, u32[]{:S(2)}, u32[]{:S(2)}) async-start(bf16[16,64,2,128]{3,0,2,1:T(8,128)(2,1)} %bitcast.20), calls=%async_computation.4 | async-start | bytes 1048576 | tf_op jit(solution)/shard_map/all_to_all | solution.py:60
  366.5 8.0 broadcast_select_fusion.5
  375.6 32.9 %scatter_fusion.4 = f32[16,129,128]{2,0,1:T(8,128)} fusion(f32[16,129,128]{2,0,1:T(8,128)} %broadcast.188.clone.1, s32[256]{0:T(256)S(1)} %bitcast.128, f32[256,16,128]{2,1,0:T(8,128)} %get-tuple-element.209), kind=kCustom, calls=%fused_computation.11 | custom fusion | flops 524288 | bytes 6292480 | tf_op jit(solution)/shard_map/scatter-add | solution.py:71
  408.5 2.3 slice.38
  410.8 10.5 all-to-all-start.4
  421.6 2.5 pad_maximum_fusion.1
  424.2 3.2 gather_fusion.3
  427.3 9.5 fusion.17
  436.9 31.4 %scatter_fusion.3 = f32[16,256,128]{2,0,1:T(8,128)} fusion(f32[16,256,128]{2,0,1:T(8,128)} %fusion.17, s32[256]{0:T(256)S(1)} %bitcast.124, f32[256,16,128]{2,1,0:T(8,128)} %get-tuple-element.208), kind=kCustom, calls=%fused_computation.10 | custom fusion | flops 524288 | bytes 6292480 | tf_op jit(solution)/shard_map/scatter-add | solution.py:67
  468.3 2.4 bitcast_select_fusion.1
  470.7 17.3 %scatter_fusion.5 = f32[16,256,128]{2,0,1:T(8,128)} fusion(f32[16,256,128]{2,0,1:T(8,128)} %scatter_fusion.3, s32[128]{0:T(128)S(1)} %reshape.144, f32[128,16,128]{2,1,0:T(8,128)} %bitcast.111), kind=kCustom, calls=%fused_computation.12 | custom fusion | flops 262144 | bytes 3146240 | tf_op jit(solution)/shard_map/scatter-add | solution.py:78
  488.0 3.1 fusion.26
  491.1 3.6 copy.43
  494.8 33.0 %reduce-scatter.6.cloned.1.call-done = f32[4,256,128]{2,1,0:T(8,128)} async-done(((f32[16,256,128]{2,1,0:T(8,128)}), f32[4,256,128]{2,1,0:T(8,128)}) %reduce-scatter.6.cloned.1.call-update) | async-done | bytes 524304 | tf_op jit(solution)/shard_map/reduce_scatter | solution.py:89
  527.9 1.3 multiply_reduce_fusion.2
  529.1 124.6 %psum.29 = f32[4]{0:T(128)S(1)} all-reduce(f32[4]{0:T(128)S(1)} %multiply_reduce_fusion.2), channel_id=1, replica_groups=mesh['curve'=64,'band'=4] {'curve'}, use_global_device_ids=true, to_apply=%region_15.16 | all-reduce | flops 4 | bytes 32 | tf_op jit(solution)/shard_map/psum | solution.py:102
  653.7 1.3 multiply_reduce_fusion.1
  655.0 128.5 %psum.30 = f32[4]{0:T(128)S(1)} all-reduce(f32[4]{0:T(128)S(1)} %multiply_reduce_fusion.1), channel_id=1, replica_groups=mesh['curve'=64,'band'=4] {'curve'}, use_global_device_ids=true, to_apply=%region_17.18 | all-reduce | flops 4 | bytes 32 | tf_op jit(solution)/shard_map/psum | solution.py:104
  784.3 17.9 %all-gather.8.cloned.1.call-done = bf16[16,256,128]{2,1,0:T(8,128)(2,1)} async-done(((bf16[4,256,128]{2,1,0:T(8,128)(2,1)}), bf16[16,256,128]{2,1,0:T(8,128)(2,1)}) %all-gather.8.cloned.1.call-update) | async-done | bytes 1048592 | tf_op jit(solution)/shard_map/all_gather | solution.py:88
  802.2 2.9 copy.45
  805.1 2.7 gather_fusion.4
  807.8 11.8 %all-to-all-start.5 = ((bf16[16,64,2,128]{3,0,2,1:T(8,128)(2,1)}), bf16[16,64,2,128]{3,0,2,1:T(8,128)(2,1)}, u32[]{:S(2)}, u32[]{:S(2)}) async-start(bf16[16,64,2,128]{3,0,2,1:T(8,128)(2,1)} %bitcast.115), calls=%async_computation.7 | async-start | bytes 1048576 | tf_op jit(solution)/shard_map/all_to_all | solution.py:60
  819.6 8.0 broadcast_select_fusion.4
  828.6 32.9 %scatter_fusion.7 = f32[16,129,128]{2,0,1:T(8,128)} fusion(f32[16,129,128]{2,0,1:T(8,128)} %broadcast.188, s32[256]{0:T(256)S(1)} %bitcast.129, f32[256,16,128]{2,1,0:T(8,128)} %get-tuple-element.211), kind=kCustom, calls=%fused_computation.14 | custom fusion | flops 524288 | bytes 6292480 | tf_op jit(solution)/shard_map/scatter-add | solution.py:71
  861.5 2.3 slice.39
  863.8 10.6 all-to-all-start.6
  874.7 2.7 pad_maximum_fusion.2
  877.4 3.2 gather_fusion.5
  880.6 9.6 fusion.20
  890.2 31.4 %scatter_fusion.6 = f32[16,256,128]{2,0,1:T(8,128)} fusion(f32[16,256,128]{2,0,1:T(8,128)} %fusion.20, s32[256]{0:T(256)S(1)} %bitcast.125, f32[256,16,128]{2,1,0:T(8,128)} %get-tuple-element.210), kind=kCustom, calls=%fused_computation.13 | custom fusion | flops 524288 | bytes 6292480 | tf_op jit(solution)/shard_map/scatter-add | solution.py:67
  921.6 2.5 bitcast_select_fusion
  924.1 16.4 %scatter_fusion.8 = f32[16,256,128]{2,0,1:T(8,128)} fusion(f32[16,256,128]{2,0,1:T(8,128)} %scatter_fusion.6, s32[128]{0:T(128)S(1)} %reshape.144, f32[128,16,128]{2,1,0:T(8,128)} %bitcast.109), kind=kCustom, calls=%fused_computation.15 | custom fusion | flops 262144 | bytes 3146240 | tf_op jit(solution)/shard_map/scatter-add | solution.py:78
  940.4 3.1 fusion.28
  943.6 3.6 copy.48
  947.2 32.4 %reduce-scatter.8.cloned.1.call-done = f32[4,256,128]{2,1,0:T(8,128)} async-done(((f32[16,256,128]{2,1,0:T(8,128)}), f32[4,256,128]{2,1,0:T(8,128)}) %reduce-scatter.8.cloned.1.call-update) | async-done | bytes 524304 | tf_op jit(solution)/shard_map/reduce_scatter | solution.py:89
  979.6 1.3 multiply_reduce_fusion
  980.9 124.6 %psum.31 = f32[4]{0:T(128)S(1)} all-reduce(f32[4]{0:T(128)S(1)} %multiply_reduce_fusion), channel_id=1, replica_groups=mesh['curve'=64,'band'=4] {'curve'}, use_global_device_ids=true, to_apply=%region_23.24 | all-reduce | flops 4 | bytes 32 | tf_op jit(solution)/shard_map/psum | solution.py:109
  1105.5 1.2 while.20
  1106.7 2.1 multiply_add_fusion
  (76 shorter events, 9.1 us)
Async XLA Ops:
  6.5 153.6 %copy-start = (bf16[64,128,128]{2,1,0:T(8,128)(2,1)S(1)}, bf16[64,128,128]{2,1,0:T(8,128)(2,1)}, u32[]{:S(2)}) copy-start(bf16[64,128,128]{2,1,0:T(8,128)(2,1)} %param.8) | copy-start | bytes 6291460
  6.5 32.1 %all-gather.4.cloned.1.call-start = ((), (), s32[]{:S(2)}) async-start(), calls=%async_computation.10 | async-start | bytes 1310720 | tf_op jit(solution)/shard_map/all_gather | solution.py:88
  35.6 18.2 %copy-start.5 = (s32[256,1]{0,1:T(1,128)S(1)}, s32[256,1]{0,1:T(1,128)}, u32[]{:S(2)}) copy-start(s32[256,1]{0,1:T(1,128)} %param.9) | copy-start | bytes 3076
  40.5 21.3 %copy-start.3 = (bf16[16,256,128]{2,0,1:T(8,128)(2,1)}, bf16[16,256,128]{2,0,1:T(8,128)(2,1)S(1)}, u32[]{:S(2)}) copy-start(bf16[16,256,128]{2,0,1:T(8,128)(2,1)S(1)} %copy.35) | copy-start | bytes 3145732
  42.0 41.7 %all-to-all-start.1 = ((bf16[16,64,2,128]{3,0,2,1:T(8,128)(2,1)}), bf16[16,64,2,128]{3,0,2,1:T(8,128)(2,1)}, u32[]{:S(2)}, u32[]{:S(2)}) async-start(bf16[16,64,2,128]{3,0,2,1:T(8,128)(2,1)} %bitcast.116), calls=%async_computation.1 | async-start | bytes 1048576 | tf_op jit(solution)/shard_map/all_to_all | solution.py:60
  83.7 11.2 %copy-start.4 = (bf16[16,256,128]{2,0,1:T(8,128)(2,1)S(1)}, bf16[16,256,128]{2,0,1:T(8,128)(2,1)}, u32[]{:S(2)}) copy-start(bf16[16,256,128]{2,0,1:T(8,128)(2,1)} %copy-done.3) | copy-start | bytes 3145732
  83.7 57.7 %all-to-all-start.2 = ((f32[16,64,2,128]{3,0,2,1:T(8,128)}), f32[16,64,2,128]{3,0,2,1:T(8,128)}, u32[]{:S(2)}, u32[]{:S(2)}) async-start(f32[16,64,2,128]{3,0,2,1:T(8,128)} %bitcast.112), calls=%async_computation.2 | async-start | bytes 2097152 | tf_op jit(solution)/shard_map/all_to_all | solution.py:74
  94.3 104.9 %reduce-scatter.4.cloned.1.call-start = ((), (), s32[]{:S(2)}) async-start(), calls=%async_computation.11 | async-start | bytes 2621440 | tf_op jit(solution)/shard_map/reduce_scatter | solution.py:89
  166.7 32.6 %copy-start.2 = (f32[4,256,128]{2,1,0:T(8,128)S(1)}, f32[4,256,128]{2,1,0:T(8,128)}, u32[]{:S(2)}) copy-start(f32[4,256,128]{2,1,0:T(8,128)} %param.6) | copy-start | bytes 1572868
  166.8 182.6 %all-gather.6.cloned.1.call-start = ((), (), s32[]{:S(2)}) async-start(), calls=%async_computation.12 | async-start | bytes 1310720 | tf_op jit(solution)/shard_map/all_gather | solution.py:88
  354.9 55.9 %all-to-all-start.3 = ((bf16[16,64,2,128]{3,0,2,1:T(8,128)(2,1)}), bf16[16,64,2,128]{3,0,2,1:T(8,128)(2,1)S(1)}, u32[]{:S(2)}, u32[]{:S(2)}) async-start(bf16[16,64,2,128]{3,0,2,1:T(8,128)(2,1)} %bitcast.20), calls=%async_computation.4 | async-start | bytes 1048576 | tf_op jit(solution)/shard_map/all_to_all | solution.py:60
  410.8 57.5 %all-to-all-start.4 = ((f32[16,64,2,128]{3,0,2,1:T(8,128)}), f32[16,64,2,128]{3,0,2,1:T(8,128)}, u32[]{:S(2)}, u32[]{:S(2)}) async-start(f32[16,64,2,128]{3,0,2,1:T(8,128)} %bitcast.114), calls=%async_computation.5 | async-start | bytes 2097152 | tf_op jit(solution)/shard_map/all_to_all | solution.py:74
  421.4 106.5 %reduce-scatter.6.cloned.1.call-start = ((), (), s32[]{:S(2)}) async-start(), calls=%async_computation.13 | async-start | bytes 2621440 | tf_op jit(solution)/shard_map/reduce_scatter | solution.py:89
  494.8 307.4 %all-gather.8.cloned.1.call-start = ((), (), s32[]{:S(2)}) async-start(), calls=%async_computation.14 | async-start | bytes 1310720 | tf_op jit(solution)/shard_map/all_gather | solution.py:88
  527.9 255.6 %copy-start.1 = (f32[4,256,128]{2,1,0:T(8,128)S(1)}, f32[4,256,128]{2,1,0:T(8,128)}, u32[]{:S(2)}) copy-start(f32[4,256,128]{2,1,0:T(8,128)} %reduce-scatter.6.cloned.1.call-done) | copy-start | bytes 1572868
  807.8 56.0 %all-to-all-start.5 = ((bf16[16,64,2,128]{3,0,2,1:T(8,128)(2,1)}), bf16[16,64,2,128]{3,0,2,1:T(8,128)(2,1)}, u32[]{:S(2)}, u32[]{:S(2)}) async-start(bf16[16,64,2,128]{3,0,2,1:T(8,128)(2,1)} %bitcast.115), calls=%async_computation.7 | async-start | bytes 1048576 | tf_op jit(solution)/shard_map/all_to_all | solution.py:60
  863.8 57.8 %all-to-all-start.6 = ((f32[16,64,2,128]{3,0,2,1:T(8,128)}), f32[16,64,2,128]{3,0,2,1:T(8,128)}, u32[]{:S(2)}, u32[]{:S(2)}) async-start(f32[16,64,2,128]{3,0,2,1:T(8,128)} %bitcast.113), calls=%async_computation.8 | async-start | bytes 2097152 | tf_op jit(solution)/shard_map/all_to_all | solution.py:74
  874.4 105.2 %reduce-scatter.8.cloned.1.call-start = ((), (), s32[]{:S(2)}) async-start(), calls=%async_computation.15 | async-start | bytes 2621440 | tf_op jit(solution)/shard_map/reduce_scatter | solution.py:89
Sparse Core Ops, SparseCore 0:
  9.2 29.3 all-gather.3
  166.9 32.3 reduce-scatter.3
  327.1 22.1 all-gather.5
  494.9 32.9 reduce-scatter.5
  784.4 17.6 all-gather.7
  947.3 32.2 reduce-scatter.7
where the time goes:
time: 1120 us
  blocking collectives  524 us (47%)
  other arithmetic  261 us (23%)
  waiting for transfers between devices  141 us (13%)
  starting transfers between devices  67.8 us (6%)
  matrix products  61.9 us (6%)
  local copies, waits for them, and re-layouts  44.8 us (4%)
  between operations  13.7 us (1%)
    psum x1, blocking collectives, body(): rest_norm = lax.psum(jnp.sum(rest * rest, axis=(1, 2)), 'curve')  128 us
    psum x1, blocking collectives, body(): lax.psum(jnp.sum(second * image_second, axis=(1, 2)), 'curve')  125 us
    psum x1, blocking collectives, body(): alpha_first = lax.psum(jnp.sum(first * image, axis=(1, 2)), 'curve')  125 us
    psum x1, blocking collectives, body(): drive_norm = lax.psum(jnp.sum(drive * drive, axis=(1, 2)), 'curve')  125 us
    reduce_scatter x3, waiting for transfers between devices, operate(): lax.psum_scatter(local_product(whole, blocks, diag_blocks, plan), 'band',...  97.9 us
    scatter-add x3, other arithmetic, local_product(): result = result.at[:, target, :].add(kept)  94.3 us
    scatter-add x3, other arithmetic, local_product(): outgoing = jnp.zeros((vectors, groups * CAP + 1, node_count), jnp.float32...  86.5 us
    scatter-add x3, other arithmetic, local_product(): result = result.at[:, asked_index, :].add(returned)  50 us
  transfers between devices with their start and end apart: 12, of which 6 were waited for; matrix products, arithmetic and copies ran while one was open for 24% of the time, Pallas kernels for 0%

commit v1 on v0

v1 whole, which is shorter than its diff:
```python
import functools

import jax
import jax.numpy as jnp
from jax import lax
from jax.experimental import pallas as pl
from jax.experimental.pallas import tpu as pltpu
from jax.sharding import PartitionSpec as P

CAP = 2
TAYLOR = 16
APPS = 3
GROUPS = 4

epsilon = 1e-06
time_step = 0.5
quadratic = 1.0

F32 = jnp.float32
BF16 = jnp.bfloat16


def phi_weights(alpha_first, beta_first, alpha_second):
    term_one = jnp.ones_like(alpha_first)
    term_two = jnp.zeros_like(alpha_first)
    total_one, total_two = term_one, term_two
    for turn in range(1, TAYLOR):
        factor = time_step / (turn + 1.0)
        next_one = factor * (alpha_first * term_one + beta_first * term_two)
        next_two = factor * (beta_first * term_one + alpha_second * term_two)
        term_one, term_two = next_one, next_two
        total_one, total_two = total_one + next_one, total_two + next_two
    return total_one, total_two


def kernel(
    curve,
    state_ref,
    col_ref,
    row_ref,
    blocks_hbm,
    diag_hbm,
    out_ref,
    blocks,
    diag,
    slabs,
    staging,
    pool,
    outbox,
    inbox,
    mirrored,
    forward,
    ret_out,
    ret_in,
    share,
    relay_in,
    sum_in,
    first,
    rest,
    onehot,
    ask_out,
    ask_in,
    index_vmem,
    index_smem,
    quad,
    band_in,
    total_out,
    total_in,
    load_sem,
    ask_sem,
    index_sem,
    slab_send,
    slab_recv,
    gather_sem,
    return_sem,
    sum_send,
    sum_recv,
    band_sem,
    total_sem,
):
    per, rows, nodes = state_ref.shape
    vectors = per * GROUPS
    half = per // 2
    slots = curve * CAP
    quarter = diag.shape[0]
    me = lax.axis_index("curve")
    band = lax.axis_index("band")
    shift = rows.bit_length() - 1

    def other(step):
        return lax.rem(band + step, GROUPS)

    def peer(step):
        return lax.rem(me + step, curve)

    def load(chunk_ref, buffer, n):
        return pltpu.make_async_copy(chunk_ref, buffer, load_sem.at[n])

    load(blocks_hbm, blocks, 0).start()
    load(diag_hbm, diag, 1).start()

    barrier = pltpu.get_barrier_semaphore()

    @pl.loop(1, curve)
    def _(step):
        pl.semaphore_signal(barrier, inc=1, device_id={"curve": peer(step)})

    for step in range(1, GROUPS):
        pl.semaphore_signal(barrier, inc=1, device_id={"band": other(step)})

    own_col = lax.shift_right_logical(col_ref[...], shift)
    own_row = lax.shift_right_logical(row_ref[...], shift)
    tgt_row = row_ref[...] & (rows - 1)
    remote_row = own_row != me
    sub = lax.broadcasted_iota(jnp.int32, (rows, rows), 0)
    lane = lax.broadcasted_iota(jnp.int32, (rows, rows), 1)
    same = own_col == own_row
    rank_row = jnp.sum((same & (sub < lane)).astype(jnp.int32), axis=0, keepdims=True)
    rank_col = jnp.sum((same & (lane < sub)).astype(jnp.int32), axis=1, keepdims=True)
    bucket_col = jnp.where(own_col != me, own_col * CAP + rank_col, -1)
    pick_row = jnp.where(remote_row, rows + own_row * CAP + rank_row, tgt_row)
    padded = jnp.where(remote_row, own_row * 8 + rank_row, -1)
    place = lax.broadcasted_iota(jnp.int32, (curve * 8, rows), 0)
    wanted = jnp.sum(jnp.where(place == padded, tgt_row + 1, 0), axis=1, keepdims=True)
    ask_out[...] = jnp.broadcast_to(wanted, ask_out.shape)
    ask_in[pl.ds(pl.multiple_of(me * 8, 8), 8), :] = jnp.zeros((8, ask_in.shape[1]), jnp.int32)
    lane_slot = lax.broadcasted_iota(jnp.int32, (rows, slots), 1)
    source = lax.broadcasted_iota(jnp.int32, (rows, slots), 0)
    row_of = jnp.sum(jnp.where(bucket_col == lane_slot, source, 0), axis=0, keepdims=True)
    index_vmem[0:1, 0:rows] = jnp.clip(pick_row, 0, rows + slots - 1)
    index_vmem[1:2, 0:slots] = jnp.clip(row_of, 0, rows - 1)
    onehot[:, 0:rows] = ((tgt_row == sub) & ~remote_row).astype(F32).astype(BF16)

    pl.semaphore_wait(barrier, curve - 1 + GROUPS - 1)

    def ask_copy(target, own):
        return pltpu.make_async_remote_copy(
            src_ref=ask_out.at[pl.ds(pl.multiple_of(target * 8, 8), 8)],
            dst_ref=ask_in.at[pl.ds(pl.multiple_of(own * 8, 8), 8)],
            send_sem=ask_sem.at[0],
            recv_sem=ask_sem.at[1],
            device_id={"curve": target},
        )

    @pl.loop(1, curve)
    def _(step):
        ask_copy(peer(step), me).start()

    def wait_all(buffer, size, send, recv, wait_send):
        view = buffer.at[pl.ds(0, (curve - 1) * size)]
        copy = pltpu.make_async_remote_copy(
            src_ref=view, dst_ref=view, send_sem=send, recv_sem=recv, device_id={"curve": peer(1)}
        )
        if wait_send:
            copy.wait_send()
        else:
            copy.wait_recv()

    def take_asked():
        wait_all(ask_in, 8, ask_sem.at[0], ask_sem.at[1], False)
        place = lax.broadcasted_iota(jnp.int32, (curve * 8, slots), 0)
        slot = lax.broadcasted_iota(jnp.int32, (curve * 8, slots), 1)
        chosen = place == lax.shift_right_logical(slot, 1) * 8 + (slot & 1)
        asked = jnp.sum(jnp.where(chosen, ask_in[:, 0:slots], 0), axis=0, keepdims=True)
        index_vmem[2:3, 0:slots] = jnp.clip(asked - 1, 0, rows - 1)
        sub = lax.broadcasted_iota(jnp.int32, (rows, slots), 0)
        onehot[:, rows:] = (asked - 1 == sub).astype(F32).astype(BF16)
        copy = pltpu.make_async_copy(index_vmem, index_smem, index_sem)
        copy.start()
        copy.wait()
        wait_all(ask_out, 8, ask_sem.at[0], ask_sem.at[1], True)

    def slab_copy(app, src, dst, planes, step, n):
        return pltpu.make_async_remote_copy(
            src_ref=slabs.at[app, src, planes],
            dst_ref=slabs.at[app, dst, planes],
            send_sem=slab_send.at[app, n],
            recv_sem=slab_recv.at[app, n],
            device_id={"band": other(step)},
        )

    def interleave(app, group):
        for t in range(per):
            v = group * per + t
            staging[pl.ds(v, rows, stride=vectors), :] = slabs[app, group, t].astype(F32)

    low, high, every = pl.ds(0, half), pl.ds(half, half), pl.ds(0, per)

    def exchange_band(app, field):
        for t in range(per):
            slabs[app, 0, t] = field[t].astype(BF16)
        right = slab_copy(app, 0, 3, every, 1, 0)
        left = slab_copy(app, 0, 1, every, GROUPS - 1, 1)
        right.start()
        left.start()
        interleave(app, 0)
        right.wait_recv()
        on_right = slab_copy(app, 3, 2, low, 1, 2)
        on_right.start()
        left.wait_recv()
        on_left = slab_copy(app, 1, 2, high, GROUPS - 1, 3)
        on_left.start()
        interleave(app, 3)
        interleave(app, 1)
        on_right.wait_recv()
        on_left.wait_recv()
        interleave(app, 2)
        for copy in (right, left, on_right, on_left):
            copy.wait_send()

        @pl.loop(0, rows // 16)
        def _(n):
            piece = pl.ds(pl.multiple_of(n * 16 * vectors, 256), 16 * vectors)
            pool[pl.ds(pl.multiple_of(n * 16, 16), 16)] = (
                staging[piece, :].astype(BF16).reshape(16, vectors, nodes)
            )

    def tile(n):
        return pl.ds(pl.multiple_of(n * vectors, 16), vectors)

    wide = CAP * vectors

    def send_gather(app):
        @pl.loop(1, curve)
        def _(step):
            target = peer(step)
            for k in range(CAP):
                n = target * CAP + k
                outbox[tile(n), :] = pool[index_smem[2, n]]
            pltpu.make_async_remote_copy(
                src_ref=outbox.at[pl.ds(pl.multiple_of(target * wide, wide), wide)],
                dst_ref=inbox.at[app, pl.ds(pl.multiple_of(me * wide, wide), wide)],
                send_sem=gather_sem.at[app, 0],
                recv_sem=gather_sem.at[app, 1],
                device_id={"curve": target},
            ).start()

    def take_gather(app):
        wait_all(inbox.at[app], wide, gather_sem.at[app, 0], gather_sem.at[app, 1], False)

        @pl.loop(0, slots // 8)
        def _(n):
            piece = pl.ds(pl.multiple_of(n * 8 * vectors, 128), 8 * vectors)
            pool[pl.ds(rows + n * 8, 8)] = inbox[app, piece, :].reshape(8, vectors, nodes)

        wait_all(outbox, wide, gather_sem.at[app, 0], gather_sem.at[app, 1], True)

    def mirror():
        @pl.loop(0, rows, unroll=8)
        def _(r):
            mirrored[tile(r), :] = jnp.dot(pool[r], blocks[r], preferred_element_type=F32)

    def send_return(app):
        mine = pl.ds(pl.multiple_of(me * wide, wide), wide)
        ret_in[app, mine, :] = jnp.zeros((wide, nodes), F32)

        @pl.loop(1, curve)
        def _(step):
            target = peer(step)
            for k in range(CAP):
                n = target * CAP + k
                r = index_smem[1, n]
                ret_out[tile(n), :] = jnp.dot(pool[r], blocks[r], preferred_element_type=F32)
            pltpu.make_async_remote_copy(
                src_ref=ret_out.at[pl.ds(pl.multiple_of(target * wide, wide), wide)],
                dst_ref=ret_in.at[app, mine],
                send_sem=return_sem.at[app, 0],
                recv_sem=return_sem.at[app, 1],
                device_id={"curve": target},
            ).start()

    def contract(left, right):
        return lax.dot_general(left, right, (((1,), (1,)), ((), ())), preferred_element_type=F32)

    def multiply_forward(app):
        zeros = jnp.zeros((vectors, nodes), F32)

        def one(r, total):
            product = contract(pool[index_smem[0, r]], blocks[r])
            if app < APPS - 1:
                forward[tile(r), :] = product
            if app > 0:
                total = total + product * pool[r].astype(F32)
            return total

        total = lax.fori_loop(0, rows, one, zeros, unroll=8)

        def two(q, total):
            r = band * quarter + q
            left = pool[r]
            product = contract(left, diag[q])
            if app < APPS - 1:
                forward[tile(r), :] += product
            if app > 0:
                total = total + product * left.astype(F32)
            return total

        return lax.fori_loop(0, quarter, two, 2.0 * total, unroll=8)

    def split(value):
        upper = value.astype(BF16)
        return upper, (value - upper.astype(F32)).astype(BF16)

    def add_up(app, group, t):
        v = group * per + t
        total = forward[pl.ds(v, rows, stride=vectors), :]
        for part in split(mirrored[pl.ds(v, rows, stride=vectors), :]):
            total += jnp.dot(onehot[:, 0:rows], part, preferred_element_type=F32)
        for part in split(ret_in[app, pl.ds(v, slots, stride=vectors), :]):
            total += jnp.dot(onehot[:, rows:], part, preferred_element_type=F32)
        share[group, t] = total

    def sum_copy(app, src, dst, step, n):
        return pltpu.make_async_remote_copy(
            src_ref=src,
            dst_ref=dst,
            send_sem=sum_send.at[app, n],
            recv_sem=sum_recv.at[app, n],
            device_id={"band": other(step)},
        )

    def reduce_band(app):
        wait_all(ret_in.at[app], wide, return_sem.at[app, 0], return_sem.at[app, 1], False)
        up, down = 1, GROUPS - 1
        for t in range(half):
            add_up(app, 2, t)
        relay_up = sum_copy(app, share.at[2, low], relay_in.at[app, 0], up, 0)
        relay_up.start()
        for t in range(half, per):
            add_up(app, 2, t)
        relay_down = sum_copy(app, share.at[2, high], relay_in.at[app, 1], down, 1)
        relay_down.start()
        for t in range(half, per):
            add_up(app, 1, t)
        direct_up = sum_copy(app, share.at[1, high], sum_in.at[app, 0, high], up, 2)
        direct_up.start()
        for t in range(half):
            add_up(app, 3, t)
        direct_down = sum_copy(app, share.at[3, low], sum_in.at[app, 1, low], down, 3)
        direct_down.start()
        for t in range(half):
            add_up(app, 1, t)
        relay_up.wait_recv()
        share[1, 0:half] += relay_in[app, 0]
        last_up = sum_copy(app, share.at[1, low], sum_in.at[app, 0, low], up, 4)
        last_up.start()
        for t in range(half, per):
            add_up(app, 3, t)
        relay_down.wait_recv()
        share[3, half:per] += relay_in[app, 1]
        last_down = sum_copy(app, share.at[3, high], sum_in.at[app, 1, high], down, 5)
        last_down.start()
        for t in range(per):
            add_up(app, 0, t)
        copies = (relay_up, relay_down, direct_up, direct_down, last_up, last_down)
        for copy in copies[2:]:
            copy.wait_recv()
        for t in range(per):
            share[0, t] = share[0, t] + (sum_in[app, 0, t] + sum_in[app, 1, t])
        for copy in copies:
            copy.wait_send()
        wait_all(ret_out, wide, return_sem.at[app, 0], return_sem.at[app, 1], True)

    def send_quad(n, total):
        quad[...] = jnp.zeros_like(quad)
        for group in range(GROUPS):
            quad[group, 0:per, :] = total[group * per : (group + 1) * per, :]
        for step in range(1, GROUPS):
            pltpu.make_async_remote_copy(
                src_ref=quad.at[step],
                dst_ref=band_in.at[n, step],
                send_sem=band_sem.at[n, 0, step],
                recv_sem=band_sem.at[n, 1, step],
                device_id={"band": other(step)},
            ).start()

    def take_quad(n):
        total = quad[0]
        for step in range(1, GROUPS):
            copy = pltpu.make_async_remote_copy(
                src_ref=quad.at[step],
                dst_ref=band_in.at[n, step],
                send_sem=band_sem.at[n, 0, step],
                recv_sem=band_sem.at[n, 1, step],
                device_id={"band": other(step)},
            )
            copy.wait_recv()
            total = total + band_in[n, step]
            copy.wait_send()
        return total[0:per]

    def send_total(n, parts):
        total_out[n] = jnp.zeros_like(total_out[n])
        for k, part in enumerate(parts):
            total_out[n, k * per : (k + 1) * per, :] = part
        mine = pl.ds(pl.multiple_of(me * 16, 16), 16)
        total_in[n, mine, :] = total_out[n]

        @pl.loop(1, curve)
        def _(step):
            pltpu.make_async_remote_copy(
                src_ref=total_out.at[n],
                dst_ref=total_in.at[n, mine],
                send_sem=total_sem.at[n, 0],
                recv_sem=total_sem.at[n, 1],
                device_id={"curve": peer(step)},
            ).start()

    def take_total(n):
        wait_all(total_in.at[n], 16, total_sem.at[n, 0], total_sem.at[n, 1], False)
        total = jnp.sum(total_in[n].reshape(curve, 16, nodes), axis=0)
        wait_all(total_in.at[n], 16, total_sem.at[n, 0], total_sem.at[n, 1], True)
        total = jnp.broadcast_to(jnp.sum(total, axis=1, keepdims=True), total.shape)
        return [total[k * per : (k + 1) * per] for k in range(4)]

    def over_rows(values):
        return jnp.concatenate([jnp.sum(value, axis=0, keepdims=True) for value in values], axis=0)

    exchange_band(0, state_ref)
    take_asked()
    send_gather(0)
    load(blocks_hbm, blocks, 0).wait()
    send_return(0)
    mirror()
    load(diag_hbm, diag, 1).wait()
    take_gather(0)
    multiply_forward(0)
    reduce_band(0)
    norms = []
    for t in range(per):
        field = state_ref[t]
        drive = share[0, t] + (quadratic * field * field - field * field * field)
        first[t] = drive
        norms.append(drive * drive)
    send_total(0, [over_rows(norms)])
    norm_zero = take_total(0)[0]
    beta_zero = jnp.sqrt(norm_zero + epsilon)
    for t in range(per):
        first[t] = first[t] / beta_zero[t : t + 1]

    exchange_band(1, first)
    send_gather(1)
    send_return(1)
    mirror()
    take_gather(1)
    send_quad(0, multiply_forward(1))
    send_total(1, [take_quad(0)])
    reduce_band(1)
    alpha_first = take_total(1)[0]
    norms, along = [], []
    for t in range(per):
        value = share[0, t] - alpha_first[t : t + 1] * first[t]
        rest[t] = value
        norms.append(value * value)
        along.append(value * first[t])
    rest_norm = over_rows(norms)
    rest_along = over_rows(along)
    exchange_band(2, rest)
    send_gather(2)
    take_gather(2)
    send_quad(1, multiply_forward(2))
    send_total(2, [rest_norm, rest_along, take_quad(1)])
    norm, dot, form, _ = take_total(2)
    squared = norm + epsilon
    beta_first = jnp.sqrt(squared)
    alpha_second = form / squared - dot
    weight_one, weight_two = phi_weights(alpha_first, beta_first, alpha_second)
    scale_one = time_step * beta_zero * weight_one
    scale_two = time_step * beta_zero * weight_two / beta_first
    for t in range(per):
        out_ref[t] = state_ref[t] + (
            scale_one[t : t + 1] * first[t] + scale_two[t : t + 1] * rest[t]
        )


def body(state, blocks, diag_blocks, block_cols):
    per, rows, nodes = state.shape
    curve = lax.axis_size("curve")
    vectors = per * GROUPS
    slots = curve * CAP
    half = per // 2
    quarter = diag_blocks.shape[0]
    dma = pltpu.SemaphoreType.DMA
    vmem = pl.BlockSpec(memory_space=pltpu.VMEM)
    anywhere = pl.BlockSpec(memory_space=pl.ANY)
    return pl.pallas_call(
        functools.partial(kernel, curve),
        out_shape=jax.ShapeDtypeStruct(state.shape, F32),
        in_specs=[vmem, vmem, vmem, anywhere, anywhere],
        out_specs=vmem,
        scratch_shapes=[
            pltpu.VMEM((rows, nodes, nodes), BF16),
            pltpu.VMEM((quarter, nodes, nodes), BF16),
            pltpu.VMEM((APPS, GROUPS, per, rows, nodes), BF16),
            pltpu.VMEM((rows * vectors, nodes), F32),
            pltpu.VMEM((rows + slots, vectors, nodes), BF16),
            pltpu.VMEM((slots * vectors, nodes), BF16),
            pltpu.VMEM((APPS, slots * vectors, nodes), BF16),
            pltpu.VMEM((rows * vectors, nodes), F32),
            pltpu.VMEM((rows * vectors, nodes), F32),
            pltpu.VMEM((slots * vectors, nodes), F32),
            pltpu.VMEM((APPS - 1, slots * vectors, nodes), F32),
            pltpu.VMEM((GROUPS, per, rows, nodes), F32),
            pltpu.VMEM((APPS - 1, 2, half, rows, nodes), F32),
            pltpu.VMEM((APPS - 1, 2, per, rows, nodes), F32),
            pltpu.VMEM((per, rows, nodes), F32),
            pltpu.VMEM((per, rows, nodes), F32),
            pltpu.VMEM((rows, rows + slots), BF16),
            pltpu.VMEM((curve * 8, 128), jnp.int32),
            pltpu.VMEM((curve * 8, 128), jnp.int32),
            pltpu.VMEM((8, max(rows, slots, 128)), jnp.int32),
            pltpu.SMEM((8, max(rows, slots, 128)), jnp.int32),
            pltpu.VMEM((GROUPS, 8, nodes), F32),
            pltpu.VMEM((2, GROUPS, 8, nodes), F32),
            pltpu.VMEM((3, 16, nodes), F32),
            pltpu.VMEM((3, curve * 16, nodes), F32),
            dma((2,)),
            dma((2,)),
            dma,
            dma((APPS, 4)),
            dma((APPS, 4)),
            dma((APPS, 2)),
            dma((APPS - 1, 2)),
            dma((APPS - 1, 6)),
            dma((APPS - 1, 6)),
            dma((2, 2, GROUPS)),
            dma((3, 2)),
        ],
        compiler_params=pltpu.CompilerParams(
            collective_id=0, has_side_effects=True, vmem_limit_bytes=60 * 1024 * 1024
        ),
    )(state, block_cols.reshape(rows, 1), block_cols.reshape(1, rows), blocks.reshape(rows, nodes, nodes), diag_blocks)


def solution(mesh):
    return jax.shard_map(
        body,
        mesh=mesh,
        in_specs=(
            P("band", "curve", None),
            P("curve", "band", None, None),
            P(("curve", "band"), None, None),
            P("curve", "band"),
        ),
        out_specs=P("band", "curve", None),
        check_vma=False,
    )
```

time: 1120 us -> 229 us (0.20)
  blocking collectives: 524 us -> 0 us
  other arithmetic: 261 us -> 0 us
  Pallas kernels: 0 us -> 226 us
  waiting for transfers between devices: 141 us -> 0 us
  starting transfers between devices: 67.8 us -> 0 us
  matrix products: 61.9 us -> 0 us
  local copies, waits for them, and re-layouts: 44.8 us -> 3.34 us
  between operations: 13.7 us -> 0.01 us
    psum x4 -> x0, blocking collectives: 502 us -> none  [the longest x1 128 us: body(): rest_norm = lax.psum(jnp.sum(rest * rest, axis=(1, 2)), 'curve')]
    scatter-add x9 -> x0, other arithmetic: 231 us -> none  [the longest x3 94.3 us: local_product(): result = result.at[:, target, :].add(kept)]
    pallas_call x0 -> x1, Pallas kernels: none -> 226 us  [body(): pl.pallas_call(functools.partial(kernel, curve), out_shape=jax.ShapeDtype...]
    reduce_scatter x3 -> x0, waiting for transfers between devices: 97.9 us -> none  [operate(): lax.psum_scatter(local_product(whole, blocks, diag_blocks, plan), 'band',...]
    all_to_all x6 -> x0, starting transfers between devices: 66.9 us -> none  [the longest x3 35.2 us: local_product(): lax.all_to_all(reply, 'curve', split_axis=1, concat_axis=1, tiled=True)]
    dot_general x9 -> x0, matrix products: 61.9 us -> none  [the longest x3 28.7 us: local_product(): jnp.einsum('rac,vrc->vra', stored, gathered, preferred_element_type=jnp.f...]
    all_gather x3 -> x0, waiting for transfers between devices: 43.1 us -> none  [operate(): whole = lax.all_gather(vector, 'band', axis=0, tiled=True)]
    all_to_all x1 -> x0, blocking collectives: 22.2 us -> none  [routing(): lax.all_to_all(wanted[:-1].reshape(groups, CAP), 'curve', split_axis=0, c...]
  transfers between devices with their start and end apart: 12 -> 0, of which waited for: 6 -> 0; matrix products, arithmetic and copies ran while one was open for 24% -> 0% of each run, Pallas kernels for 0% -> 0%
where the time goes in v1:
time: 229 us
  Pallas kernels  226 us (99%)
  local copies, waits for them, and re-layouts  3.34 us (1%)
    pallas_call x1, Pallas kernels, body(): pl.pallas_call(functools.partial(kernel, curve), out_shape=jax.ShapeDtype...  226 us

profile of v1, /device:TPU:1, one launch (start us, length us, event | category | flops | bytes accessed | tf_op | source)
XLA Modules:
  0.0 229.0 jit_solution(15511299356417148947)
XLA Ops:
  0.0 1.5 copy.5.col_ref
  1.5 225.7 %shard_map.46 = f32[4,256,128]{2,1,0:T(8,128)} custom-call(f32[4,256,128]{2,1,0:T(8,128)} %state_ref.1, s32[256,1]{1,0:T(8,128)} %copy.5.col_ref, s32[1,256]{1,0:T(1,128)} %bitcast.3, bf16[256,128,128]{2,1,0:T(8,128)(2,1)} %bitcast.2, bf16[64,128,128]{2,1,0:T(8,128)(2,1)} %diag_hbm.1), custom_call_target="tpu_custom_call" | custom-call | tf_op jit(solution)/shard_map/pallas_call | solution.py:486
  227.1 1.9 copy.7

commit v2 on v1

--- a/solution.py
+++ b/solution.py
@@ -33,6 +33,11 @@
     return total_one, total_two
 
 
+def extents(curve):
+    deep = curve // 8 if curve >= 16 else curve // 2
+    return deep, curve // deep
+
+
 def kernel(
     curve,
     state_ref,
@@ -42,6 +47,7 @@
     diag_hbm,
     out_ref,
     blocks,
+    turned,
     diag,
     slabs,
     staging,
@@ -65,6 +71,8 @@
     quad,
     band_in,
     total_out,
+    total_mid,
+    total_two,
     total_in,
     load_sem,
     ask_sem,
@@ -86,6 +94,7 @@
     me = lax.axis_index("curve")
     band = lax.axis_index("band")
     shift = rows.bit_length() - 1
+    deep, broad = extents(curve)
 
     def other(step):
         return lax.rem(band + step, GROUPS)
@@ -142,9 +151,20 @@
             device_id={"curve": target},
         )
 
-    @pl.loop(1, curve)
-    def _(step):
-        ask_copy(peer(step), me).start()
+    share_of = rows // curve
+
+    def send_asked():
+        def turn(r):
+            turned[r] = blocks[r].T
+
+        @pl.loop(1, curve)
+        def _(step):
+            ask_copy(peer(step), me).start()
+            for k in range(share_of):
+                turn(step * share_of + k)
+
+        for k in range(share_of):
+            turn(k)
 
     def wait_all(buffer, size, send, recv, wait_send):
         view = buffer.at[pl.ds(0, (curve - 1) * size)]
@@ -186,13 +206,14 @@
 
     low, high, every = pl.ds(0, half), pl.ds(half, half), pl.ds(0, per)
 
-    def exchange_band(app, field):
+    def exchange_band(app, field, between=lambda: None):
         for t in range(per):
             slabs[app, 0, t] = field[t].astype(BF16)
         right = slab_copy(app, 0, 3, every, 1, 0)
         left = slab_copy(app, 0, 1, every, GROUPS - 1, 1)
         right.start()
         left.start()
+        between()
         interleave(app, 0)
         right.wait_recv()
         on_right = slab_copy(app, 3, 2, low, 1, 2)
@@ -220,6 +241,9 @@
 
     wide = CAP * vectors
 
+    def mirror(r):
+        mirrored[tile(r), :] = jnp.dot(pool[r], blocks[r], preferred_element_type=F32)
+
     def send_gather(app):
         @pl.loop(1, curve)
         def _(step):
@@ -227,6 +251,9 @@
             for k in range(CAP):
                 n = target * CAP + k
                 outbox[tile(n), :] = pool[index_smem[2, n]]
+            if app < APPS - 1:
+                for k in range(share_of):
+                    mirror(step * share_of + k)
             pltpu.make_async_remote_copy(
                 src_ref=outbox.at[pl.ds(pl.multiple_of(target * wide, wide), wide)],
                 dst_ref=inbox.at[app, pl.ds(pl.multiple_of(me * wide, wide), wide)],
@@ -235,6 +262,10 @@
                 device_id={"curve": target},
             ).start()
 
+        if app < APPS - 1:
+            for k in range(share_of):
+                mirror(k)
+
     def take_gather(app):
         wait_all(inbox.at[app], wide, gather_sem.at[app, 0], gather_sem.at[app, 1], False)
 
@@ -244,11 +275,6 @@
             pool[pl.ds(rows + n * 8, 8)] = inbox[app, piece, :].reshape(8, vectors, nodes)
 
         wait_all(outbox, wide, gather_sem.at[app, 0], gather_sem.at[app, 1], True)
-
-    def mirror():
-        @pl.loop(0, rows, unroll=8)
-        def _(r):
-            mirrored[tile(r), :] = jnp.dot(pool[r], blocks[r], preferred_element_type=F32)
 
     def send_return(app):
         mine = pl.ds(pl.multiple_of(me * wide, wide), wide)
@@ -269,33 +295,30 @@
                 device_id={"curve": target},
             ).start()
 
-    def contract(left, right):
-        return lax.dot_general(left, right, (((1,), (1,)), ((), ())), preferred_element_type=F32)
-
     def multiply_forward(app):
         zeros = jnp.zeros((vectors, nodes), F32)
 
         def one(r, total):
-            product = contract(pool[index_smem[0, r]], blocks[r])
+            product = jnp.dot(pool[index_smem[0, r]], turned[r], preferred_element_type=F32)
             if app < APPS - 1:
                 forward[tile(r), :] = product
             if app > 0:
                 total = total + product * pool[r].astype(F32)
             return total
 
-        total = lax.fori_loop(0, rows, one, zeros, unroll=8)
+        total = lax.fori_loop(0, rows, one, zeros, unroll=min(rows, 32))
 
         def two(q, total):
             r = band * quarter + q
             left = pool[r]
-            product = contract(left, diag[q])
+            product = jnp.dot(left, diag[q], preferred_element_type=F32)
             if app < APPS - 1:
                 forward[tile(r), :] += product
             if app > 0:
                 total = total + product * left.astype(F32)
             return total
 
-        return lax.fori_loop(0, quarter, two, 2.0 * total, unroll=8)
+        return lax.fori_loop(0, quarter, two, 2.0 * total, unroll=min(quarter, 16))
 
     def split(value):
         upper = value.astype(BF16)
@@ -303,12 +326,12 @@
 
     def add_up(app, group, t):
         v = group * per + t
-        total = forward[pl.ds(v, rows, stride=vectors), :]
-        for part in split(mirrored[pl.ds(v, rows, stride=vectors), :]):
-            total += jnp.dot(onehot[:, 0:rows], part, preferred_element_type=F32)
-        for part in split(ret_in[app, pl.ds(v, slots, stride=vectors), :]):
-            total += jnp.dot(onehot[:, rows:], part, preferred_element_type=F32)
-        share[group, t] = total
+        here = mirrored[pl.ds(v, rows, stride=vectors), :]
+        returned = ret_in[app, pl.ds(v, slots, stride=vectors), :]
+        parts = jnp.concatenate(split(jnp.concatenate([here, returned], axis=0)), axis=1)
+        both = jnp.dot(onehot[...], parts, preferred_element_type=F32)
+        own = forward[pl.ds(v, rows, stride=vectors), :]
+        share[group, t] = own + (both[:, 0:nodes] + both[:, nodes:])
 
     def sum_copy(app, src, dst, step, n):
         return pltpu.make_async_remote_copy(
@@ -319,7 +342,7 @@
             device_id={"band": other(step)},
         )
 
-    def reduce_band(app):
+    def reduce_band(app, early=lambda: None, late=lambda: None):
         wait_all(ret_in.at[app], wide, return_sem.at[app, 0], return_sem.at[app, 1], False)
         up, down = 1, GROUPS - 1
         for t in range(half):
@@ -338,6 +361,7 @@
             add_up(app, 3, t)
         direct_down = sum_copy(app, share.at[3, low], sum_in.at[app, 1, low], down, 3)
         direct_down.start()
+        early()
         for t in range(half):
             add_up(app, 1, t)
         relay_up.wait_recv()
@@ -350,6 +374,7 @@
         share[3, half:per] += relay_in[app, 1]
         last_down = sum_copy(app, share.at[3, high], sum_in.at[app, 1, high], down, 5)
         last_down.start()
+        late()
         for t in range(per):
             add_up(app, 0, t)
         copies = (relay_up, relay_down, direct_up, direct_down, last_up, last_down)
@@ -393,36 +418,71 @@
         total_out[n] = jnp.zeros_like(total_out[n])
         for k, part in enumerate(parts):
             total_out[n, k * per : (k + 1) * per, :] = part
-        mine = pl.ds(pl.multiple_of(me * 16, 16), 16)
-        total_in[n, mine, :] = total_out[n]
-
-        @pl.loop(1, curve)
-        def _(step):
+        total_stage(n, 0)
+
+    def total_peer(stage, step):
+        if stage == 0:
+            z = lax.rem(me, 2 * deep) // 2
+            return me + 2 * (lax.rem(z + step, deep) - z)
+        wide = (me // (2 * deep)) * 2 + lax.rem(me, 2)
+        there = lax.rem(wide + step, broad)
+        return (there // 2) * 2 * deep + me % (2 * deep) // 2 * 2 + lax.rem(there, 2)
+
+    def total_buffers(n, stage):
+        if stage == 0:
+            return total_out.at[n], total_mid.at[n], deep, lax.rem(me, 2 * deep) // 2
+        mine = (me // (2 * deep)) * 2 + lax.rem(me, 2)
+        return total_two.at[n], total_in.at[n], broad, mine
+
+    def total_stage(n, stage):
+        source, target, count, slot = total_buffers(n, stage)
+        mine = pl.ds(pl.multiple_of(slot * 16, 16), 16)
+        target[mine, :] = source[...]
+        for step in range(1, count):
             pltpu.make_async_remote_copy(
-                src_ref=total_out.at[n],
-                dst_ref=total_in.at[n, mine],
-                send_sem=total_sem.at[n, 0],
-                recv_sem=total_sem.at[n, 1],
-                device_id={"curve": peer(step)},
+                src_ref=source,
+                dst_ref=target.at[mine],
+                send_sem=total_sem.at[n, stage, 0],
+                recv_sem=total_sem.at[n, stage, 1],
+                device_id={"curve": total_peer(stage, step)},
             ).start()
 
+    def total_wait(n, stage):
+        _, target, count, _ = total_buffers(n, stage)
+        view = target.at[pl.ds(0, (count - 1) * 16)]
+        copy = pltpu.make_async_remote_copy(
+            src_ref=view,
+            dst_ref=view,
+            send_sem=total_sem.at[n, stage, 0],
+            recv_sem=total_sem.at[n, stage, 1],
+            device_id={"curve": total_peer(stage, 1)},
+        )
+        copy.wait_recv()
+        total = jnp.sum(target[...].reshape(count, 16, nodes), axis=0)
+        copy.wait_send()
+        return total
+
+    def pass_total(n):
+        total_two[n] = total_wait(n, 0)
+        total_stage(n, 1)
+
     def take_total(n):
-        wait_all(total_in.at[n], 16, total_sem.at[n, 0], total_sem.at[n, 1], False)
-        total = jnp.sum(total_in[n].reshape(curve, 16, nodes), axis=0)
-        wait_all(total_in.at[n], 16, total_sem.at[n, 0], total_sem.at[n, 1], True)
+        total = total_wait(n, 1)
         total = jnp.broadcast_to(jnp.sum(total, axis=1, keepdims=True), total.shape)
         return [total[k * per : (k + 1) * per] for k in range(4)]
 
     def over_rows(values):
         return jnp.concatenate([jnp.sum(value, axis=0, keepdims=True) for value in values], axis=0)
 
-    exchange_band(0, state_ref)
+    def ask():
+        load(blocks_hbm, blocks, 0).wait()
+        load(diag_hbm, diag, 1).wait()
+        send_asked()
+
+    exchange_band(0, state_ref, ask)
     take_asked()
     send_gather(0)
-    load(blocks_hbm, blocks, 0).wait()
     send_return(0)
-    mirror()
-    load(diag_hbm, diag, 1).wait()
     take_gather(0)
     multiply_forward(0)
     reduce_band(0)
@@ -433,6 +493,7 @@
         first[t] = drive
         norms.append(drive * drive)
     send_total(0, [over_rows(norms)])
+    pass_total(0)
     norm_zero = take_total(0)[0]
     beta_zero = jnp.sqrt(norm_zero + epsilon)
     for t in range(per):
@@ -441,11 +502,9 @@
     exchange_band(1, first)
     send_gather(1)
     send_return(1)
-    mirror()
     take_gather(1)
     send_quad(0, multiply_forward(1))
-    send_total(1, [take_quad(0)])
-    reduce_band(1)
+    reduce_band(1, lambda: send_total(1, [take_quad(0)]), lambda: pass_total(1))
     alpha_first = take_total(1)[0]
     norms, along = [], []
     for t in range(per):
@@ -460,6 +519,7 @@
     take_gather(2)
     send_quad(1, multiply_forward(2))
     send_total(2, [rest_norm, rest_along, take_quad(1)])
+    pass_total(2)
     norm, dot, form, _ = take_total(2)
     squared = norm + epsilon
     beta_first = jnp.sqrt(squared)
@@ -480,6 +540,7 @@
     slots = curve * CAP
     half = per // 2
     quarter = diag_blocks.shape[0]
+    deep, broad = extents(curve)
     dma = pltpu.SemaphoreType.DMA
     vmem = pl.BlockSpec(memory_space=pltpu.VMEM)
     anywhere = pl.BlockSpec(memory_space=pl.ANY)
@@ -489,6 +550,7 @@
         in_specs=[vmem, vmem, vmem, anywhere, anywhere],
         out_specs=vmem,
         scratch_shapes=[
+            pltpu.VMEM((rows, nodes, nodes), BF16),
             pltpu.VMEM((rows, nodes, nodes), BF16),
             pltpu.VMEM((quarter, nodes, nodes), BF16),
             pltpu.VMEM((APPS, GROUPS, per, rows, nodes), BF16),
@@ -513,7 +575,9 @@
             pltpu.VMEM((GROUPS, 8, nodes), F32),
             pltpu.VMEM((2, GROUPS, 8, nodes), F32),
             pltpu.VMEM((3, 16, nodes), F32),
-            pltpu.VMEM((3, curve * 16, nodes), F32),
+            pltpu.VMEM((3, deep * 16, nodes), F32),
+            pltpu.VMEM((3, 16, nodes), F32),
+            pltpu.VMEM((3, broad * 16, nodes), F32),
             dma((2,)),
             dma((2,)),
             dma,
@@ -524,7 +588,7 @@
             dma((APPS - 1, 6)),
             dma((APPS - 1, 6)),
             dma((2, 2, GROUPS)),
-            dma((3, 2)),
+            dma((3, 2, 2)),
         ],
         compiler_params=pltpu.CompilerParams(
             collective_id=0, has_side_effects=True, vmem_limit_bytes=60 * 1024 * 1024

time: 229 us -> 210 us (0.917)
  Pallas kernels: 226 us -> 207 us
    pallas_call x1, Pallas kernels: 226 us -> 207 us  [body(): pl.pallas_call(functools.partial(kernel, curve), out_shape=jax.ShapeDtype...]
where the time goes in v2:
time: 210 us
  Pallas kernels  207 us (99%)
  local copies, waits for them, and re-layouts  3.34 us (2%)
    pallas_call x1, Pallas kernels, body(): pl.pallas_call(functools.partial(kernel, curve), out_shape=jax.ShapeDtype...  207 us

profile of v2, /device:TPU:1, one launch (start us, length us, event | category | flops | bytes accessed | tf_op | source)
XLA Modules:
  0.0 210.3 jit_solution(7822120571397924774)
XLA Ops:
  0.0 1.5 copy.5.col_ref
  1.5 207.0 %shard_map.46 = f32[4,256,128]{2,1,0:T(8,128)} custom-call(f32[4,256,128]{2,1,0:T(8,128)} %state_ref.1, s32[256,1]{1,0:T(8,128)} %copy.5.col_ref, s32[1,256]{1,0:T(1,128)} %bitcast.3, bf16[256,128,128]{2,1,0:T(8,128)(2,1)} %bitcast.2, bf16[64,128,128]{2,1,0:T(8,128)(2,1)} %diag_hbm.1), custom_call_target="tpu_custom_call" | custom-call | tf_op jit(solution)/shard_map/pallas_call | solution.py:547
  208.5 1.9 copy.7

commit v3 on v2

--- a/solution.py
+++ b/solution.py
@@ -58,6 +58,8 @@
     forward,
     ret_out,
     ret_in,
+    ret_out_two,
+    ret_in_two,
     share,
     relay_in,
     sum_in,
@@ -199,10 +201,12 @@
             device_id={"band": other(step)},
         )
 
+    def position(group, t):
+        return (group * per + t - per - half) % vectors
+
     def interleave(app, group):
         for t in range(per):
-            v = group * per + t
-            staging[pl.ds(v, rows, stride=vectors), :] = slabs[app, group, t].astype(F32)
+            staging[pl.ds(position(group, t), rows, stride=vectors), :] = slabs[app, group, t].astype(F32)
 
     low, high, every = pl.ds(0, half), pl.ds(half, half), pl.ds(0, per)
 
@@ -276,24 +280,54 @@
 
         wait_all(outbox, wide, gather_sem.at[app, 0], gather_sem.at[app, 1], True)
 
+    part_rows = vectors // 2
+    pair = CAP * part_rows
+
+    def return_buffers(app):
+        return (ret_out, ret_in) if app == 0 else (ret_out_two, ret_in_two)
+
+    def return_copy(app, part, target):
+        source, arrived = return_buffers(app)
+        return pltpu.make_async_remote_copy(
+            src_ref=source.at[part, pl.ds(pl.multiple_of(target * pair, pair), pair)],
+            dst_ref=arrived.at[part, pl.ds(pl.multiple_of(me * pair, pair), pair)],
+            send_sem=return_sem.at[app, part, 0],
+            recv_sem=return_sem.at[app, part, 1],
+            device_id={"curve": target},
+        )
+
     def send_return(app):
-        mine = pl.ds(pl.multiple_of(me * wide, wide), wide)
-        ret_in[app, mine, :] = jnp.zeros((wide, nodes), F32)
+        source, arrived = return_buffers(app)
+        mine = pl.ds(pl.multiple_of(me * pair, pair), pair)
+        for part in range(2):
+            arrived[part, mine, :] = jnp.zeros((pair, nodes), arrived.dtype)
 
         @pl.loop(1, curve)
         def _(step):
             target = peer(step)
+            products = []
             for k in range(CAP):
-                n = target * CAP + k
-                r = index_smem[1, n]
-                ret_out[tile(n), :] = jnp.dot(pool[r], blocks[r], preferred_element_type=F32)
-            pltpu.make_async_remote_copy(
-                src_ref=ret_out.at[pl.ds(pl.multiple_of(target * wide, wide), wide)],
-                dst_ref=ret_in.at[app, mine],
-                send_sem=return_sem.at[app, 0],
-                recv_sem=return_sem.at[app, 1],
-                device_id={"curve": target},
-            ).start()
+                r = index_smem[1, target * CAP + k]
+                products.append(jnp.dot(pool[r], blocks[r], preferred_element_type=F32))
+            there = pl.ds(pl.multiple_of(target * pair, pair), pair)
+            for part in range(2):
+                own = [value[part * part_rows : (part + 1) * part_rows] for value in products]
+                source[part, there, :] = jnp.concatenate(own, axis=0).astype(source.dtype)
+            return_copy(app, 0, target).start()
+
+        @pl.loop(1, curve)
+        def _(step):
+            return_copy(app, 1, peer(step)).start()
+
+    def take_return(app, part):
+        source, arrived = return_buffers(app)
+        sems = (return_sem.at[app, part, 0], return_sem.at[app, part, 1])
+        wait_all(arrived.at[part], pair, *sems, False)
+
+    def end_return(app, part):
+        source, _ = return_buffers(app)
+        sems = (return_sem.at[app, part, 0], return_sem.at[app, part, 1])
+        wait_all(source.at[part], pair, *sems, True)
 
     def multiply_forward(app):
         zeros = jnp.zeros((vectors, nodes), F32)
@@ -325,9 +359,10 @@
         return upper, (value - upper.astype(F32)).astype(BF16)
 
     def add_up(app, group, t):
-        v = group * per + t
+        v = position(group, t)
         here = mirrored[pl.ds(v, rows, stride=vectors), :]
-        returned = ret_in[app, pl.ds(v, slots, stride=vectors), :]
+        arrived = return_buffers(app)[1]
+        returned = arrived[v // part_rows, pl.ds(v % part_rows, slots, stride=part_rows), :]
         parts = jnp.concatenate(split(jnp.concatenate([here, returned], axis=0)), axis=1)
         both = jnp.dot(onehot[...], parts, preferred_element_type=F32)
         own = forward[pl.ds(v, rows, stride=vectors), :]
@@ -343,7 +378,7 @@
         )
 
     def reduce_band(app, early=lambda: None, late=lambda: None):
-        wait_all(ret_in.at[app], wide, return_sem.at[app, 0], return_sem.at[app, 1], False)
+        take_return(app, 0)
         up, down = 1, GROUPS - 1
         for t in range(half):
             add_up(app, 2, t)
@@ -362,6 +397,7 @@
         direct_down = sum_copy(app, share.at[3, low], sum_in.at[app, 1, low], down, 3)
         direct_down.start()
         early()
+        take_return(app, 1)
         for t in range(half):
             add_up(app, 1, t)
         relay_up.wait_recv()
@@ -384,12 +420,15 @@
             share[0, t] = share[0, t] + (sum_in[app, 0, t] + sum_in[app, 1, t])
         for copy in copies:
             copy.wait_send()
-        wait_all(ret_out, wide, return_sem.at[app, 0], return_sem.at[app, 1], True)
+        end_return(app, 0)
+        end_return(app, 1)
 
     def send_quad(n, total):
         quad[...] = jnp.zeros_like(quad)
         for group in range(GROUPS):
-            quad[group, 0:per, :] = total[group * per : (group + 1) * per, :]
+            for t in range(0, per, half):
+                v = position(group, t)
+                quad[group, t : t + half, :] = total[v : v + half, :]
         for step in range(1, GROUPS):
             pltpu.make_async_remote_copy(
                 src_ref=quad.at[step],
@@ -560,8 +599,10 @@
             pltpu.VMEM((APPS, slots * vectors, nodes), BF16),
             pltpu.VMEM((rows * vectors, nodes), F32),
             pltpu.VMEM((rows * vectors, nodes), F32),
-            pltpu.VMEM((slots * vectors, nodes), F32),
-            pltpu.VMEM((APPS - 1, slots * vectors, nodes), F32),
+            pltpu.VMEM((2, slots * vectors // 2, nodes), F32),
+            pltpu.VMEM((2, slots * vectors // 2, nodes), F32),
+            pltpu.VMEM((2, slots * vectors // 2, nodes), F32),
+            pltpu.VMEM((2, slots * vectors // 2, nodes), F32),
             pltpu.VMEM((GROUPS, per, rows, nodes), F32),
             pltpu.VMEM((APPS - 1, 2, half, rows, nodes), F32),
             pltpu.VMEM((APPS - 1, 2, per, rows, nodes), F32),
@@ -584,7 +625,7 @@
             dma((APPS, 4)),
             dma((APPS, 4)),
             dma((APPS, 2)),
-            dma((APPS - 1, 2)),
+            dma((APPS - 1, 2, 2)),
             dma((APPS - 1, 6)),
             dma((APPS - 1, 6)),
             dma((2, 2, GROUPS)),

time: 210 us -> 192 us (0.914)
  Pallas kernels: 207 us -> 188 us
    pallas_call x1, Pallas kernels: 207 us -> 188 us  [body(): pl.pallas_call(functools.partial(kernel, curve), out_shape=jax.ShapeDtype...]
where the time goes in v3:
time: 192 us
  Pallas kernels  188 us (98%)
  local copies, waits for them, and re-layouts  3.34 us (2%)
    pallas_call x1, Pallas kernels, body(): pl.pallas_call(functools.partial(kernel, curve), out_shape=jax.ShapeDtype...  188 us

profile of v3, /device:TPU:1, one launch (start us, length us, event | category | flops | bytes accessed | tf_op | source)
XLA Modules:
  0.0 191.6 jit_solution(8299174176512045214)
XLA Ops:
  0.0 1.5 copy.5.col_ref
  1.5 188.3 %shard_map.46 = f32[4,256,128]{2,1,0:T(8,128)} custom-call(f32[4,256,128]{2,1,0:T(8,128)} %state_ref.1, s32[256,1]{1,0:T(8,128)} %copy.5.col_ref, s32[1,256]{1,0:T(1,128)} %bitcast.3, bf16[256,128,128]{2,1,0:T(8,128)(2,1)} %bitcast.2, bf16[64,128,128]{2,1,0:T(8,128)(2,1)} %diag_hbm.1), custom_call_target="tpu_custom_call" | custom-call | tf_op jit(solution)/shard_map/pallas_call | solution.py:586
  189.7 1.9 copy.7
